TPU v7x, 768 devices: a whole 4x8x12 slice. The times are simulated.
768 devices in a mesh: grp: 96 (over x, z, core), own: 8 (over y).
Axes of the slice: x: 4, y: 8, z: 12, core: 2. Of those that a mesh axis runs over, the one named last changes fastest.
Arguments:
- lookup_slot: int32 [98304, 26], P(('grp', 'own')), may hold values from 0 to 5119, as said below
- emb_cot: bfloat16 [98304, 26, 128], P(('grp', 'own')), may hold values from -0.796875 to 0.796875
- slot_row: int32 [768, 1024], P(('grp', 'own')), may hold values from 0 to 2047, as said below
- slot_count: int32 [768, 8], P(('grp', 'own')), may hold values from 32 to 128, as said below
- bottom_act: bfloat16 [98304, 256], P(('grp', 'own')), may hold values from -6 to 6
- bottom_cot: bfloat16 [98304, 128], P(('grp', 'own')), may hold values from -0.039794922 to 0.039794922
Outputs:
- freq_grad: float32 [4096, 128], replicated
- table_grad: float32 [1572864, 128], P(('grp', 'own'))
- weight_grad: float32 [256, 128], replicated
- bias_grad: float32 [128], replicated
Inputs may be any that keep to these rules, and one draw needn't show every extreme that they name: `slot_count`: each device sends its owners between 32 and 128 slots; in every group one owner, drawn from the seed, receives exactly 128 from every device of the group, and one device, drawn from the seed, sends exactly 128 to every owner. `slot_row`: within one device the live slots for one owner name distinct rows; slots past the device's total are 0 and no lookup names them. `lookup_slot`: every live slot of a device is named by one or more of its lookups; infrequent values stay below 4096 plus the device's total of slot_count.
All inputs are finite; a program needn't handle non-finite values.
Results may differ from a plain program's by a relative error of at most 0.0003.
Values sent between devices are 32-bit elements; how exact they have to be, the bound alone decides.
A program may use at most 32 MiB of HBM per device.

v0:
```python
import jax
import jax.numpy as jnp
from jax import lax
from jax.sharding import PartitionSpec as P

FREQ = 4096
ROWS_OWN = 2048


def slot_position(packed, slot_ends, starts, capacity):
    owner_of = jnp.sum((packed[:, None] >= slot_ends[None, :]).astype(jnp.int32), axis=1)
    picks = owner_of[:, None] == jnp.arange(slot_ends.shape[0], dtype=jnp.int32)[None, :]
    first_slot = jnp.sum(jnp.where(picks, starts[None, :], 0), axis=1)
    return owner_of * capacity + packed - first_slot


def per_device(lookup_slot, emb_cot, slot_row, slot_count, bottom_act, bottom_cot):
    emb_width = emb_cot.shape[2]
    lookups = lookup_slot.shape[0] * lookup_slot.shape[1]
    lookup_ids = lookup_slot.reshape(lookups)
    rows_cot = emb_cot.reshape(lookups, emb_width)
    counts = slot_count[0]
    peer_count = counts.shape[0]
    total_slots = slot_row.shape[1]
    capacity = total_slots // peer_count
    slot_ends = jnp.cumsum(counts)
    starts = slot_ends - counts
    target = jnp.where(
        lookup_ids < FREQ,
        lookup_ids,
        FREQ + slot_position(lookup_ids - FREQ, slot_ends, starts, capacity),
    )
    columns = FREQ + total_slots
    block_cols = 512

    def block_sum(block_index):
        labels = block_index * block_cols + jnp.arange(block_cols, dtype=jnp.int32)
        picks = (target[:, None] == labels[None, :]).astype(jnp.bfloat16)
        return lax.dot_general(
            picks, rows_cot, (((0,), (0,)), ((), ())), preferred_element_type=jnp.float32
        )

    block_sums = lax.map(block_sum, jnp.arange(columns // block_cols, dtype=jnp.int32)).reshape(
        columns, emb_width
    )
    freq_local = block_sums[:FREQ]
    slot_grads = block_sums[FREQ:].reshape(peer_count, capacity, emb_width)
    positions = jnp.arange(total_slots, dtype=jnp.int32)
    owner_pos = positions // capacity
    within = positions % capacity
    is_live = within < counts[owner_pos]
    packed = jnp.clip(starts[owner_pos] + within, 0, total_slots - 1)
    dest_rows = (
        jnp.where(is_live, slot_row[0][packed], 0).astype(jnp.float32).reshape(peer_count, capacity)
    )
    weight_part = lax.dot_general(
        bottom_act, bottom_cot, (((0,), (0,)), ((), ())), preferred_element_type=jnp.float32
    )
    bias_part = jnp.sum(bottom_cot.astype(jnp.float32), axis=0)
    freq_grad, weight_grad, bias_grad = lax.psum(
        (freq_local, weight_part, bias_part), ("grp", "own")
    )
    received, dest_in = (
        lax.all_to_all(slot_grads, "own", split_axis=0, concat_axis=0, tiled=True),
        lax.all_to_all(dest_rows, "own", split_axis=0, concat_axis=0, tiled=True),
    )
    flat_rows = received.reshape(total_slots, emb_width)
    flat_dest = dest_in.reshape(total_slots).astype(jnp.int32)
    table_grad = jnp.zeros((ROWS_OWN, emb_width), jnp.float32).at[flat_dest].add(flat_rows)
    return (freq_grad, table_grad, weight_grad, bias_grad)


def solution(mesh):
    placed = (
        P(("grp", "own"), None),
        P(("grp", "own"), None, None),
        P(("grp", "own"), None),
        P(("grp", "own"), None),
        P(("grp", "own"), None),
        P(("grp", "own"), None),
    )
    return jax.shard_map(
        per_device,
        mesh=mesh,
        in_specs=placed,
        out_specs=(P(), P(("grp", "own"), None), P(), P()),
        check_vma=False,
    )
```

profile of v0, /device:TPU:1, one launch (start us, length us, event | category | flops | bytes accessed | tf_op | source)
XLA Modules:
  0.0 561.5 jit_solution(16384673732887066408)
XLA Ops:
  7.2 0.8 copy.13
  8.2 0.8 reduce-window.4
  9.0 0.7 fusion.16
  9.9 1.7 copy.14
  11.9 44.0 %while.10 = (s32[]{:T(128)}, f32[10,512,128]{2,1,0:T(8,128)}, s32[3328]{0:T(1024)S(1)}, s32[10]{0:T(128)S(1)}, bf16[3328,128]{1,0:T(8,128)(2,1)S(1)}, /*index=5*/s32[]{:T(128)}, s32[1]{0:T(128)}) while((s32[]{:T(128)}, f32[10,512,128]{2,1,0:T(8,128)}, s32[3328]{0:T(1024)S(1)}, s32[10]{0:T(128)S(1)}, bf16[3328,128]{1,0:T(8,128)(2,1)S(1)}, ...), condition=%wide.region_4.5_spmd, body=%wide.region_3.4_spmd.sunk | while | flops 437912064 | bytes 1132137 | solution.py:43
  13.2 3.1 fusion.28
  17.6 3.1 fusion.28
  22.0 3.1 fusion.28
  26.3 3.2 fusion.28
  30.7 3.2 fusion.28
  35.2 3.2 fusion.28
  39.6 3.1 fusion.28
  44.0 3.2 fusion.28
  48.3 3.2 fusion.28
  52.8 3.1 fusion.28
  55.9 3.1 slice.10
  59.0 0.9 fusion.19
  59.9 0.7 fusion.17
  60.6 0.7 fusion.18
  61.3 4.2 compare_select_fusion.8
  65.5 4.5 compare_select_fusion.7
  70.0 1.3 broadcast_select_fusion.1
  71.3 4.5 gather_fusion
  76.5 7.7 %all-to-all-start = ((f32[8,1,128]{2,1,0:T(1,128)}), f32[8,1,128]{2,1,0:T(1,128)S(1)}, u32[]{:S(2)}, u32[]{:S(2)}) async-start(f32[8,1,128]{2,1,0:T(1,128)} %fusion.15), calls=%async_computation | async-start | bytes 8192 | tf_op jit(solution)/shard_map/all_to_all | solution.py:65
  84.1 1.9 slice.12
  86.0 4.7 all-to-all-done
  90.7 3.5 all-to-all-start.1
  94.2 121.9 %psum.23 = f32[128]{0:T(128)} all-reduce(f32[128]{0:T(128)S(1)} %convert_reduce_fusion.1), channel_id=1, replica_groups=mesh['grp'=96,'own'=8] {'grp','own'}, use_global_device_ids=true, to_apply=%region_9.10 | all-reduce | flops 128 | bytes 1024 | tf_op jit(solution)/shard_map/psum | solution.py:60
  216.1 7.5 %scatter_custom_fusion = f32[2048,128]{1,0:T(8,128)} fusion(s32[1024]{0:T(1024)S(1)} %bitcast.64, f32[1024,128]{1,0:T(8,128)S(1)} %bitcast.56, f32[]{:T(128)} %constant.56.clone.1), kind=kCustom, calls=%fused_computation.9 | custom fusion | flops 131072 | bytes 1048580 | tf_op jit(solution)/shard_map/scatter-add | solution.py:69
  223.5 327.4 %all-reduce.3.cloned.1.call-done = (f32[4096,128]{1,0:T(8,128)}, f32[256,128]{1,0:T(8,128)}) async-done(((f32[4096,128]{1,0:T(8,128)}, f32[256,128]{1,0:T(8,128)}), (f32[4096,128]{1,0:T(8,128)}, f32[256,128]{1,0:T(8,128)})) %all-reduce.3.cloned.1.call-update) | async-done | bytes 2228240 | tf_op jit(solution)/shard_map/psum | solution.py:60
  550.9 3.1 copy.26
  554.0 0.7 copy.27
  (48 shorter events, 7.3 us)
Async XLA Ops:
  7.2 51.8 %copy-start = (bf16[128,256]{1,0:T(8,128)(2,1)S(1)}, bf16[128,256]{1,0:T(8,128)(2,1)}, u32[]{:S(2)}) copy-start(bf16[128,256]{1,0:T(8,128)(2,1)} %param.12) | copy-start | bytes 196612
  7.2 543.7 %all-reduce.3.cloned.1.call-start = ((), (), s32[]{:S(2)}) async-start(), calls=%async_computation.2 | async-start | bytes 4456448 | tf_op jit(solution)/shard_map/psum | solution.py:60
  55.9 3.1 copy-start.2
  55.9 4.0 copy-start.4
  55.9 15.4 %copy-start.1 = (s32[1,1024]{1,0:T(1,128)S(1)}, s32[1,1024]{1,0:T(1,128)}, u32[]{:S(2)}) copy-start(s32[1,1024]{1,0:T(1,128)} %param.10) | copy-start | bytes 12292
  76.5 14.2 %all-to-all-start = ((f32[8,1,128]{2,1,0:T(1,128)}), f32[8,1,128]{2,1,0:T(1,128)S(1)}, u32[]{:S(2)}, u32[]{:S(2)}) async-start(f32[8,1,128]{2,1,0:T(1,128)} %fusion.15), calls=%async_computation | async-start | bytes 8192 | tf_op jit(solution)/shard_map/all_to_all | solution.py:65
  90.7 125.4 %all-to-all-start.1 = ((f32[8,128,128]{2,1,0:T(8,128)}), f32[8,128,128]{2,1,0:T(8,128)S(1)}, u32[]{:S(2)}, u32[]{:S(2)}) async-start(f32[8,128,128]{2,1,0:T(8,128)} %bitcast.33), calls=%async_computation.1 | async-start | bytes 1048576 | tf_op jit(solution)/shard_map/all_to_all | solution.py:64
  550.9 3.1 copy-start.3
Sparse Core Ops, SparseCore 0:
  60.0 490.8 all-reduce.2
where the time goes:
time: 562 us
  waiting for transfers between devices  332 us (59%)
  blocking collectives  122 us (22%)
  matrix products  32.4 us (6%)
  local copies, waits for them, and re-layouts  23.4 us (4%)
  other arithmetic  19.9 us (4%)
  between operations  14.2 us (3%)
  starting transfers between devices  11.2 us (2%)
  loops' own time  6.61 us (1%)
    psum x1, waiting for transfers between devices, per_device(): lax.psum((freq_local, weight_part, bias_part), ('grp', 'own'))  327 us
    psum x1, blocking collectives, per_device(): lax.psum((freq_local, weight_part, bias_part), ('grp', 'own'))  122 us
    dot_general x10, matrix products, block_sum(): lax.dot_general(picks, rows_cot, (((0,), (0,)), ((), ())), preferred_elem...  31.5 us
  transfers between devices with their start and end apart: 3, of which 2 were waited for; matrix products, arithmetic and copies ran while one was open for 5% of the time, Pallas kernels for 0%

commit v1 on v0

v1 whole, which is shorter than its diff:
```python
import functools

import jax
import jax.numpy as jnp
from jax import lax
from jax.experimental import pallas as pl
from jax.experimental.pallas import tpu as pltpu
from jax.sharding import PartitionSpec as P

MESH = pl.DeviceIdType.MESH
F32 = jnp.float32
BF16 = jnp.bfloat16

NX, NY, NZ = 4, 8, 12
FREQ = 4096
EMB = 128
SLOTS = 1024
CAP = 128
ROWS_OWN = 2048
HALF = FREQ // 2
FX = HALF // NX
WX = 128 // NX
R1 = 576
R2 = R1 // NY
R3 = R2 // NZ
BLK = 256
VMEM_LIMIT = 40 * 2**20


def nearest_last(n):
    return sorted(range(1, n), key=lambda d: -min(d, n - d))


def onehot_bf16(rows_rel, iota_bf):
    return jnp.where(iota_bf == rows_rel, jnp.ones((), BF16), jnp.zeros((), BF16))


def relative(ids, base, size):
    rel = ids - base
    ok = (rel >= 0) & (rel < size)
    return jnp.where(ok, rel, -1).astype(F32).astype(BF16)


def main_kernel(
    ids_ref, emb_ref, slot_row_ref, counts_ref, act_ref, cot_ref,
    g_ref, table_ref,
    rhs, hi_s, part, rc, rx, s1, ry, s2z, rz, gz, t72, wsc, sg, ra, ssem, rsem,
):
    g = lax.axis_index("grp")
    y = lax.axis_index("own")
    x = g // (2 * NZ)
    z = (g // 2) % NZ
    c = g % 2

    def dev(xx, yy, zz, cc):
        return (xx * (2 * NZ) + zz * 2 + cc, yy)

    def to_x(d):
        return dev((x + d) % NX, y, z, c)

    def to_y(d):
        return dev(x, (y + d) % NY, z, c)

    def to_z(d):
        return dev(x, y, (z + d) % NZ, c)

    to_c = dev(x, y, z, 1 - c)

    used = [0]

    def copy(src, dst, target):
        i = used[0]
        used[0] += 1
        cp = pltpu.make_async_remote_copy(
            src_ref=src, dst_ref=dst, send_sem=ssem.at[i], recv_sem=rsem.at[i],
            device_id=target, device_id_type=MESH,
        )
        cp.start()
        return cp

    order_x, order_y, order_z = nearest_last(NX), nearest_last(NY), nearest_last(NZ)
    barrier = pltpu.get_barrier_semaphore()
    peers = [to_c] + [to_x(d) for d in order_x] + [to_y(d) for d in order_y] + [to_z(d) for d in order_z]
    for p in peers:
        pl.semaphore_signal(barrier, inc=1, device_id=p, device_id_type=MESH)

    counts = [counts_ref[0, p] for p in range(NY)]
    ends, total = [], 0
    for p in range(NY):
        total = total + counts[p]
        ends.append(total)
    starts = [e - n for e, n in zip(ends, counts)]
    ids = ids_ref[...]
    packed = ids - FREQ
    slot = packed
    for p in range(NY - 1):
        slot = slot + jnp.where(packed >= ends[p], CAP - counts[p], 0)
    freq = ids < FREQ
    hi_s[...] = jnp.where(freq, ids & (HALF - 1), HALF + (slot & (SLOTS // 2 - 1)))
    lo = jnp.where(freq, ids >> 11, slot >> 9).astype(F32)
    nf = ids.shape[0]
    for f in range(nf):
        col = jnp.transpose(jnp.broadcast_to(lo[f : f + 1, :], (128, 128)))
        v = emb_ref[f * 128 : (f + 1) * 128, :]
        right = v * col.astype(BF16)
        rhs[f * 128 : (f + 1) * 128, 0:128] = v * (1.0 - col).astype(BF16)
        rhs[f * 128 : (f + 1) * 128, 128:256] = right

    cot = cot_ref[...]
    wsc[...] = lax.dot_general(act_ref[...], cot, (((0,), (0,)), ((), ())), preferred_element_type=F32)
    bias = jnp.sum(cot.astype(F32), axis=0, keepdims=True)

    iota_bf = lax.broadcasted_iota(jnp.int32, (BLK, 128), 0).astype(F32).astype(BF16)

    def block_sum(base):
        rel = relative(hi_s[...], base, BLK)
        lhs = jnp.concatenate([onehot_bf16(rel[f : f + 1, :], iota_bf) for f in range(nf)], axis=1)
        return jnp.dot(lhs, rhs[...], preferred_element_type=F32)

    order = order_x + [0]
    c_copies = []
    x_copies = []

    def after_core(k):
        o = order[k]
        c_copies[k].wait()
        rc[o] = rc[o] + part[c, o]
        if o != 0:
            x_copies.append(copy(rc.at[o], rx.at[o - 1], to_x(o)))

    for k, o in enumerate(order):
        px = (x + o) % NX

        @pl.loop(0, FX // BLK)
        def _(b, o=o, px=px):
            acc = block_sum(px * FX + b * BLK)
            at = pl.ds(pl.multiple_of(b * BLK, BLK), BLK)
            part[0, o, at, :] = acc[:, 0:128]
            part[1, o, at, :] = acc[:, 128:256]

        for h in range(2):
            part[h, o, FX : FX + WX, :] = wsc[pl.ds(pl.multiple_of(h * 128 + px * WX, WX), WX), :]
            part[h, o, FX + WX : FX + WX + 8, :] = jnp.broadcast_to(bias, (8, 128))
            part[h, o, FX + WX + 8 : R1, :] = jnp.zeros((R1 - FX - WX - 8, 128), F32)
        if k == 0:
            pl.semaphore_wait(barrier, len(peers))
        c_copies.append(copy(part.at[1 - c, o], rc.at[o], to_c))
        if k > 0:
            after_core(k - 1)
    after_core(len(order) - 1)

    @pl.loop(0, SLOTS // 2 // BLK)
    def _(b):
        acc = block_sum(HALF + b * BLK)
        for q in range(BLK // CAP):
            sg[b * (BLK // CAP) + q, 0:CAP, :] = acc[q * CAP : (q + 1) * CAP, 0:128]
            sg[NY // 2 + b * (BLK // CAP) + q, 0:CAP, :] = acc[q * CAP : (q + 1) * CAP, 128:256]

    for cp in x_copies:
        cp.wait()
    s1[...] = (rc[0] + rx[0]) + (rx[1] + rx[2])

    def rows_y(k):
        return pl.ds(pl.multiple_of(k * R2, 8), R2)

    y_copies = [copy(s1.at[rows_y((y + d) % NY)], ry.at[d - 1], to_y(d)) for d in order_y]

    sr = jnp.broadcast_to(slot_row_ref[...], (8, SLOTS))
    which = lax.broadcasted_iota(jnp.int32, (8, SLOTS), 0)
    parts = jnp.where(which == 0, sr >> 4, sr & 15).astype(F32).astype(BF16)
    diff = lax.broadcasted_iota(jnp.int32, (SLOTS, CAP), 0) - lax.broadcasted_iota(jnp.int32, (SLOTS, CAP), 1)
    lane = lax.broadcasted_iota(jnp.int32, (8, CAP), 1)
    for p in range(NY):
        pick = jnp.where(diff == starts[p], 1.0, 0.0).astype(BF16)
        both = jnp.dot(parts, pick, preferred_element_type=F32)
        row = both[0:1, :] * 16.0 + both[1:2, :]
        row = jnp.where(lane < counts[p], jnp.broadcast_to(row, (8, CAP)), 0.0)
        sg[p, CAP : CAP + 8, :] = row

    for cp in y_copies:
        cp.wait()
    s2 = s1[rows_y(y), :]
    for d in range(1, NY):
        s2 = s2 + ry[d - 1]
    for k in range(NZ):
        s2z[k] = s2[k * R3 : (k + 1) * R3, :]

    z_copies = [copy(s2z.at[(z + d) % NZ], rz.at[d - 1], to_z(d)) for d in order_z]
    a_copies = [copy(sg.at[(y + d) % NY], ra.at[d], to_y(d)) for d in order_y]
    ra[0] = sg[y]
    for cp in z_copies:
        cp.wait()
    s3 = s2z[z]
    for d in range(1, NZ):
        s3 = s3 + rz[d - 1]
    gz[z] = s3
    zg_copies = [copy(gz.at[z], gz.at[z], to_z(d)) for d in order_z]

    for cp in a_copies:
        cp.wait()
    for d in range(NY):
        v = ra[d, 0:CAP, :]
        top = v.astype(BF16)
        rhs[d * CAP : (d + 1) * CAP, 0:128] = top
        rhs[d * CAP : (d + 1) * CAP, 128:256] = (v - top.astype(F32)).astype(BF16)

    @pl.loop(0, ROWS_OWN // BLK)
    def _(b):
        cols = []
        for d in range(NY):
            rel = relative(ra[d, CAP : CAP + 8, :].astype(jnp.int32), b * BLK, BLK)
            cols.append(onehot_bf16(rel[0:1, :], iota_bf))
        lhs = jnp.concatenate(cols, axis=1)
        acc = jnp.dot(lhs, rhs[0:SLOTS, :], preferred_element_type=F32)
        table_ref[pl.ds(pl.multiple_of(b * BLK, BLK), BLK), :] = acc[:, 0:128] + acc[:, 128:256]

    for cp in zg_copies:
        cp.wait()
    for k in range(NZ):
        t72[k * R3 : (k + 1) * R3, :] = gz[k]

    g_ref[c, x, rows_y(y), :] = t72[...]
    yg_copies = [copy(t72, g_ref.at[c, x, rows_y(y)], to_y(d)) for d in order_y]
    for cp in yg_copies:
        cp.wait()
    xg_copies = [copy(g_ref.at[c, x], g_ref.at[c, x], to_x(d)) for d in order_x]
    cg_copies = [copy(g_ref.at[c, x], g_ref.at[c, x], to_c)]
    for d, cp in zip(order_x, xg_copies):
        cp.wait_recv()
        xs = (x - d + NX) % NX
        cg_copies.append(copy(g_ref.at[c, xs], g_ref.at[c, xs], to_c))
    for cp in xg_copies:
        cp.wait_send()
    for cp in cg_copies:
        cp.wait()


N_COPIES = NX + (NX - 1) + 3 * (NY - 1) + 2 * (NZ - 1) + (NX - 1) + NX


def finish_kernel(g_ref, table_in, freq_ref, table_ref, weight_ref, bias_ref, sem):
    cps = []

    def copy(src, dst):
        cp = pltpu.make_async_copy(src, dst, sem.at[len(cps)])
        cp.start()
        cps.append(cp)

    for h in range(2):
        for k in range(NX):
            copy(g_ref.at[h, k, 0:FX], freq_ref.at[pl.ds(h * HALF + k * FX, FX)])
            copy(g_ref.at[h, k, FX : FX + WX], weight_ref.at[pl.ds(h * 128 + k * WX, WX)])
    copy(table_in, table_ref)
    bias_ref[...] = g_ref[0, 0, FX + WX : FX + WX + 1, :]
    for cp in cps:
        cp.wait()


def per_device(lookup_slot, emb_cot, slot_row, slot_count, bottom_act, bottom_cot):
    n, f = lookup_slot.shape
    ids = lookup_slot.T
    emb = jnp.transpose(emb_cot, (1, 0, 2)).reshape(f * n, EMB)
    vm = pl.BlockSpec(memory_space=pltpu.VMEM)
    sm = pl.BlockSpec(memory_space=pltpu.SMEM)
    anym = pl.BlockSpec(memory_space=pl.ANY)
    gathered, table = pl.pallas_call(
        main_kernel,
        out_shape=(pltpu.VMEM((2, NX, R1, 128), F32), pltpu.VMEM((ROWS_OWN, 128), F32)),
        in_specs=[vm, vm, vm, sm, vm, vm],
        out_specs=(vm, vm),
        scratch_shapes=[
            pltpu.VMEM((f * n, 256), BF16),
            pltpu.VMEM((f, n), jnp.int32),
            pltpu.VMEM((2, NX, R1, 128), F32),
            pltpu.VMEM((NX, R1, 128), F32),
            pltpu.VMEM((NX - 1, R1, 128), F32),
            pltpu.VMEM((R1, 128), F32),
            pltpu.VMEM((NY - 1, R2, 128), F32),
            pltpu.VMEM((NZ, R3, 128), F32),
            pltpu.VMEM((NZ - 1, R3, 128), F32),
            pltpu.VMEM((NZ, R3, 128), F32),
            pltpu.VMEM((R2, 128), F32),
            pltpu.VMEM((256, 128), F32),
            pltpu.VMEM((NY, CAP + 8, 128), F32),
            pltpu.VMEM((NY, CAP + 8, 128), F32),
            pltpu.SemaphoreType.DMA((N_COPIES,)),
            pltpu.SemaphoreType.DMA((N_COPIES,)),
        ],
        compiler_params=pltpu.CompilerParams(
            collective_id=0, has_side_effects=True, vmem_limit_bytes=VMEM_LIMIT
        ),
    )(ids, emb, slot_row, slot_count, bottom_act, bottom_cot)
    freq_grad, table_grad, weight_grad, bias_row = pl.pallas_call(
        finish_kernel,
        out_shape=(
            jax.ShapeDtypeStruct((FREQ, 128), F32),
            jax.ShapeDtypeStruct((ROWS_OWN, 128), F32),
            jax.ShapeDtypeStruct((256, 128), F32),
            jax.ShapeDtypeStruct((1, 128), F32),
        ),
        in_specs=[vm, vm],
        out_specs=(anym, anym, anym, vm),
        scratch_shapes=[pltpu.SemaphoreType.DMA((4 * NX + 1,))],
        compiler_params=pltpu.CompilerParams(vmem_limit_bytes=4 * 2**20),
    )(
        pltpu.with_memory_space_constraint(gathered, pltpu.VMEM),
        pltpu.with_memory_space_constraint(table, pltpu.VMEM),
    )
    return freq_grad, table_grad, weight_grad, bias_row.reshape(128)


def solution(mesh):
    placed = (
        P(("grp", "own"), None),
        P(("grp", "own"), None, None),
        P(("grp", "own"), None),
        P(("grp", "own"), None),
        P(("grp", "own"), None),
        P(("grp", "own"), None),
    )
    return jax.shard_map(
        per_device,
        mesh=mesh,
        in_specs=placed,
        out_specs=(P(), P(("grp", "own"), None), P(), P()),
        check_vma=False,
    )
```

time: 562 us -> 95.5 us (0.17)
  waiting for transfers between devices: 332 us -> 0 us
  blocking collectives: 122 us -> 0 us
  Pallas kernels: 0 us -> 89.7 us
  matrix products: 32.4 us -> 0 us
  other arithmetic: 19.9 us -> 0 us
  local copies, waits for them, and re-layouts: 23.4 us -> 4.8 us
  between operations: 14.2 us -> 0.65 us
  starting transfers between devices: 11.2 us -> 0 us
  loops' own time: 6.61 us -> 0 us
    psum x1 -> x0, waiting for transfers between devices: 327 us -> none  [per_device(): lax.psum((freq_local, weight_part, bias_part), ('grp', 'own'))]
    psum x1 -> x0, blocking collectives: 122 us -> none  [per_device(): lax.psum((freq_local, weight_part, bias_part), ('grp', 'own'))]
    pallas_call x0 -> x2, Pallas kernels: none -> 89.7 us  [the longest x1 87.3 us: per_device(): pl.pallas_call(main_kernel, out_shape=(pltpu.VMEM((2, NX, R1, 128), F32),...]
    dot_general x11 -> x0, matrix products: 32.4 us -> none  [the longest x10 31.5 us: block_sum(): lax.dot_general(picks, rows_cot, (((0,), (0,)), ((), ())), preferred_elem...]
    all_to_all x2 -> x0, starting transfers between devices: 11.1 us -> none  [the longest x1 7.65 us: per_device(): lax.all_to_all(dest_rows, 'own', split_axis=0, concat_axis=0, tiled=True)]
    gather x5 -> x0, other arithmetic: 10 us -> none  [the longest x3 5.77 us: per_device(): is_live = within < counts[owner_pos]]
    scatter-add x1 -> x0, other arithmetic: 7.46 us -> none  [per_device(): jnp.zeros((ROWS_OWN, emb_width), jnp.float32).at[flat_dest].add(flat_rows)]
    another operation x1 -> x0, loops' own time: 6.61 us -> none  [per_device(): lax.map(block_sum, jnp.arange(columns // block_cols, dtype=jnp.int32))]
  transfers between devices with their start and end apart: 3 -> 0, of which waited for: 2 -> 0; matrix products, arithmetic and copies ran while one was open for 5% -> 0% of each run, Pallas kernels for 0% -> 0%
where the time goes in v1:
time: 95.5 us; the launch traced here: 95.2 us
  Pallas kernels  89.7 us (94%)
  local copies, waits for them, and re-layouts  4.8 us (5%)
    pallas_call x1, Pallas kernels, per_device(): pl.pallas_call(main_kernel, out_shape=(pltpu.VMEM((2, NX, R1, 128), F32),...  87.3 us
    unnamed x12, local copies, waits for them, and re-layouts  4.8 us
    pallas_call x1, Pallas kernels, per_device(): pl.pallas_call(finish_kernel, out_shape=(jax.ShapeDtypeStruct((FREQ, 128)...  2.36 us

profile of v1, /device:TPU:1, one launch (start us, length us, event | category | flops | bytes accessed | tf_op | source)
XLA Modules:
  0.0 95.2 jit_solution(11601344530914244434)
XLA Ops:
  0.6 0.0 copy-start
  0.6 1.1 %copy-done = bf16[128,26,128]{2,0,1:T(8,128)(2,1)S(1)} copy-done((bf16[128,26,128]{2,0,1:T(8,128)(2,1)S(1)}, bf16[128,26,128]{2,0,1:T(8,128)(2,1)}, u32[]{:S(2)}) %copy-start) | copy-done | bytes 851992
  1.8 0.0 copy-start.1
  1.8 0.8 copy-done.1
  2.6 0.0 copy-start.2
  2.6 0.8 copy-done.2
  3.4 0.0 copy-start.3
  3.4 0.7 copy-done.3
  4.1 0.0 copy-start.4
  4.1 0.7 copy-done.4
  4.8 0.0 copy-start.5
  4.8 0.7 copy-done.5
  5.4 87.3 %shard_map.93 = (f32[2,4,576,128]{3,2,1,0:T(8,128)S(1)}, f32[2048,128]{1,0:T(8,128)S(1)}) custom-call(s32[26,128]{1,0:T(8,128)S(1)} %bitcast.6, bf16[3328,128]{1,0:T(8,128)(2,1)S(1)} %bitcast.5, s32[1,1024]{1,0:T(1,128)S(1)} %copy-done.4, s32[1,8]{1,0:T(1,128)S(1)} %copy-done.5, bf16[128,256]{1,0:T(8,128)(2,1)S(1)} %copy-done.1, bf16[128,128]{1,0:T(8,128)(2,1)S(1)} %copy-done.2), custom_call_target="tpu_custom_call" | custom-call | tf_op jit(solution)/shard_map/pallas_call | solution.py:266
  92.8 2.4 %shard_map.94 = (f32[4096,128]{1,0:T(8,128)}, f32[2048,128]{1,0:T(8,128)}, f32[256,128]{1,0:T(8,128)}, f32[1,128]{1,0:T(1,128)}) custom-call(f32[2,4,576,128]{3,2,1,0:T(8,128)S(1)} %get-tuple-element.10.g_ref, f32[2048,128]{1,0:T(8,128)S(1)} %get-tuple-element.11.table_in), custom_call_target="tpu_custom_call" | custom-call | tf_op jit(solution)/shard_map/pallas_call | solution.py:293
Async XLA Ops:
  0.6 1.2 %copy-start = (bf16[128,26,128]{2,0,1:T(8,128)(2,1)S(1)}, bf16[128,26,128]{2,0,1:T(8,128)(2,1)}, u32[]{:S(2)}) copy-start(bf16[128,26,128]{2,0,1:T(8,128)(2,1)} %param.7) | copy-start | bytes 2555908
  1.8 0.8 copy-start.1
  2.6 0.8 copy-start.2
  3.4 0.7 copy-start.3
  4.1 0.7 copy-start.4
  4.8 0.7 copy-start.5

commit v2 on v1

--- a/solution.py
+++ b/solution.py
@@ -42,10 +42,21 @@
 
 
 def main_kernel(
-    ids_ref, emb_ref, slot_row_ref, counts_ref, act_ref, cot_ref,
+    ids_in, emb_in, slot_row_in, counts_in, act_in, cot_in,
     g_ref, table_ref,
+    ids_ref, emb_ref, slot_row_ref, counts_ref, act_ref, cot_ref, isem,
     rhs, hi_s, part, rc, rx, s1, ry, s2z, rz, gz, t72, wsc, sg, ra, ssem, rsem,
 ):
+    loads = [
+        pltpu.make_async_copy(src, dst, isem.at[i])
+        for i, (src, dst) in enumerate((
+            (counts_in, counts_ref), (ids_in, ids_ref), (emb_in, emb_ref),
+            (cot_in, cot_ref), (act_in, act_ref), (slot_row_in, slot_row_ref),
+        ))
+    ]
+    for ld in loads:
+        ld.start()
+
     g = lax.axis_index("grp")
     y = lax.axis_index("own")
     x = g // (2 * NZ)
@@ -67,6 +78,7 @@
     to_c = dev(x, y, z, 1 - c)
 
     used = [0]
+    sends = []
 
     def copy(src, dst, target):
         i = used[0]
@@ -76,13 +88,17 @@
             device_id=target, device_id_type=MESH,
         )
         cp.start()
+        sends.append(cp)
         return cp
 
-    order_x, order_y, order_z = nearest_last(NX), nearest_last(NY), nearest_last(NZ)
+    order_x, order_y, order_z = [2, 1, 3], nearest_last(NY), nearest_last(NZ)
     barrier = pltpu.get_barrier_semaphore()
-    peers = [to_c] + [to_x(d) for d in order_x] + [to_y(d) for d in order_y] + [to_z(d) for d in order_z]
+    peers = [to_c] + [to_x(d) for d in (1, 3)] + [to_y(d) for d in order_y] + [to_z(d) for d in order_z]
     for p in peers:
         pl.semaphore_signal(barrier, inc=1, device_id=p, device_id_type=MESH)
+
+    for ld in loads:
+        ld.wait()
 
     counts = [counts_ref[0, p] for p in range(NY)]
     ends, total = [], 0
@@ -119,14 +135,20 @@
 
     order = order_x + [0]
     c_copies = []
-    x_copies = []
+    x_copies = {}
+    half_a, half_b = pl.ds(0, R1 // 2), pl.ds(R1 // 2, R1 // 2)
 
     def after_core(k):
         o = order[k]
-        c_copies[k].wait()
+        c_copies[k].wait_recv()
         rc[o] = rc[o] + part[c, o]
-        if o != 0:
-            x_copies.append(copy(rc.at[o], rx.at[o - 1], to_x(o)))
+        if o == 2:
+            x_copies[0] = copy(rc.at[2, half_a], rx.at[0], to_x(1))
+            x_copies[1] = copy(rc.at[2, half_b], rx.at[1], to_x(3))
+        if o == 1:
+            x_copies[2] = copy(rc.at[1, half_b], rx.at[2], to_x(1))
+        if o == 3:
+            x_copies[3] = copy(rc.at[3, half_a], rx.at[3], to_x(3))
 
     for k, o in enumerate(order):
         px = (x + o) % NX
@@ -156,14 +178,12 @@
             sg[b * (BLK // CAP) + q, 0:CAP, :] = acc[q * CAP : (q + 1) * CAP, 0:128]
             sg[NY // 2 + b * (BLK // CAP) + q, 0:CAP, :] = acc[q * CAP : (q + 1) * CAP, 128:256]
 
-    for cp in x_copies:
-        cp.wait()
-    s1[...] = (rc[0] + rx[0]) + (rx[1] + rx[2])
-
-    def rows_y(k):
-        return pl.ds(pl.multiple_of(k * R2, 8), R2)
-
-    y_copies = [copy(s1.at[rows_y((y + d) % NY)], ry.at[d - 1], to_y(d)) for d in order_y]
+    x_copies[0].wait_recv()
+    rc[1, half_a, :] = rc[1, half_a, :] + rx[0]
+    x_copies[4] = copy(rc.at[1, half_a], rx.at[4], to_x(1))
+    x_copies[1].wait_recv()
+    rc[3, half_b, :] = rc[3, half_b, :] + rx[1]
+    x_copies[5] = copy(rc.at[3, half_b], rx.at[5], to_x(3))
 
     sr = jnp.broadcast_to(slot_row_ref[...], (8, SLOTS))
     which = lax.broadcasted_iota(jnp.int32, (8, SLOTS), 0)
@@ -177,8 +197,18 @@
         row = jnp.where(lane < counts[p], jnp.broadcast_to(row, (8, CAP)), 0.0)
         sg[p, CAP : CAP + 8, :] = row
 
+    for i in range(2, 6):
+        x_copies[i].wait_recv()
+    s1[half_a, :] = rc[0, half_a, :] + (rx[3] + rx[4])
+    s1[half_b, :] = rc[0, half_b, :] + (rx[2] + rx[5])
+
+    def rows_y(k):
+        return pl.ds(pl.multiple_of(k * R2, 8), R2)
+
+    y_copies = [copy(s1.at[rows_y((y + d) % NY)], ry.at[d - 1], to_y(d)) for d in order_y]
+
     for cp in y_copies:
-        cp.wait()
+        cp.wait_recv()
     s2 = s1[rows_y(y), :]
     for d in range(1, NY):
         s2 = s2 + ry[d - 1]
@@ -189,15 +219,23 @@
     a_copies = [copy(sg.at[(y + d) % NY], ra.at[d], to_y(d)) for d in order_y]
     ra[0] = sg[y]
     for cp in z_copies:
-        cp.wait()
+        cp.wait_recv()
     s3 = s2z[z]
     for d in range(1, NZ):
         s3 = s3 + rz[d - 1]
     gz[z] = s3
     zg_copies = [copy(gz.at[z], gz.at[z], to_z(d)) for d in order_z]
 
+    for cp in zg_copies:
+        cp.wait_recv()
+    for k in range(NZ):
+        t72[k * R3 : (k + 1) * R3, :] = gz[k]
+
+    g_ref[c, x, rows_y(y), :] = t72[...]
+    yg_copies = [copy(t72, g_ref.at[c, x, rows_y(y)], to_y(d)) for d in order_y]
+
     for cp in a_copies:
-        cp.wait()
+        cp.wait_recv()
     for d in range(NY):
         v = ra[d, 0:CAP, :]
         top = v.astype(BF16)
@@ -214,28 +252,34 @@
         acc = jnp.dot(lhs, rhs[0:SLOTS, :], preferred_element_type=F32)
         table_ref[pl.ds(pl.multiple_of(b * BLK, BLK), BLK), :] = acc[:, 0:128] + acc[:, 128:256]
 
-    for cp in zg_copies:
-        cp.wait()
-    for k in range(NZ):
-        t72[k * R3 : (k + 1) * R3, :] = gz[k]
-
-    g_ref[c, x, rows_y(y), :] = t72[...]
-    yg_copies = [copy(t72, g_ref.at[c, x, rows_y(y)], to_y(d)) for d in order_y]
     for cp in yg_copies:
-        cp.wait()
-    xg_copies = [copy(g_ref.at[c, x], g_ref.at[c, x], to_x(d)) for d in order_x]
+        cp.wait_recv()
+
+    def pass_on(xs, rows, target):
+        return copy(g_ref.at[c, xs, rows], g_ref.at[c, xs, rows], target)
+
+    before, after, far = (x + NX - 1) % NX, (x + 1) % NX, (x + 2) % NX
+    up_a = pass_on(x, half_a, to_x(1))
+    down_b = pass_on(x, half_b, to_x(3))
+    up_b = pass_on(x, half_b, to_x(1))
+    down_a = pass_on(x, half_a, to_x(3))
     cg_copies = [copy(g_ref.at[c, x], g_ref.at[c, x], to_c)]
-    for d, cp in zip(order_x, xg_copies):
-        cp.wait_recv()
-        xs = (x - d + NX) % NX
-        cg_copies.append(copy(g_ref.at[c, xs], g_ref.at[c, xs], to_c))
-    for cp in xg_copies:
+    up_a.wait_recv()
+    far_a = pass_on(before, half_a, to_x(1))
+    down_b.wait_recv()
+    far_b = pass_on(after, half_b, to_x(3))
+    cg_copies.append(pass_on(before, half_a, to_c))
+    cg_copies.append(pass_on(after, half_b, to_c))
+    for cp, xs, rows in ((up_b, before, half_b), (down_a, after, half_a), (far_a, far, half_a), (far_b, far, half_b)):
+        cp.wait_recv()
+        cg_copies.append(pass_on(xs, rows, to_c))
+    for cp in cg_copies:
+        cp.wait_recv()
+    for cp in sends:
         cp.wait_send()
-    for cp in cg_copies:
-        cp.wait()
-
-
-N_COPIES = NX + (NX - 1) + 3 * (NY - 1) + 2 * (NZ - 1) + (NX - 1) + NX
+
+
+N_COPIES = NX + 6 + 3 * (NY - 1) + 2 * (NZ - 1) + 6 + 7
 
 
 def finish_kernel(g_ref, table_in, freq_ref, table_ref, weight_ref, bias_ref, sem):
@@ -261,19 +305,26 @@
     ids = lookup_slot.T
     emb = jnp.transpose(emb_cot, (1, 0, 2)).reshape(f * n, EMB)
     vm = pl.BlockSpec(memory_space=pltpu.VMEM)
-    sm = pl.BlockSpec(memory_space=pltpu.SMEM)
+    hbm = pl.BlockSpec(memory_space=pltpu.HBM)
     anym = pl.BlockSpec(memory_space=pl.ANY)
     gathered, table = pl.pallas_call(
         main_kernel,
         out_shape=(pltpu.VMEM((2, NX, R1, 128), F32), pltpu.VMEM((ROWS_OWN, 128), F32)),
-        in_specs=[vm, vm, vm, sm, vm, vm],
+        in_specs=[hbm] * 6,
         out_specs=(vm, vm),
         scratch_shapes=[
+            pltpu.VMEM((f, n), jnp.int32),
+            pltpu.VMEM((f * n, EMB), BF16),
+            pltpu.VMEM(slot_row.shape, jnp.int32),
+            pltpu.SMEM(slot_count.shape, jnp.int32),
+            pltpu.VMEM(bottom_act.shape, BF16),
+            pltpu.VMEM(bottom_cot.shape, BF16),
+            pltpu.SemaphoreType.DMA((6,)),
             pltpu.VMEM((f * n, 256), BF16),
             pltpu.VMEM((f, n), jnp.int32),
             pltpu.VMEM((2, NX, R1, 128), F32),
             pltpu.VMEM((NX, R1, 128), F32),
-            pltpu.VMEM((NX - 1, R1, 128), F32),
+            pltpu.VMEM((6, R1 // 2, 128), F32),
             pltpu.VMEM((R1, 128), F32),
             pltpu.VMEM((NY - 1, R2, 128), F32),
             pltpu.VMEM((NZ, R3, 128), F32),
@@ -289,7 +340,7 @@
         compiler_params=pltpu.CompilerParams(
             collective_id=0, has_side_effects=True, vmem_limit_bytes=VMEM_LIMIT
         ),
-    )(ids, emb, slot_row, slot_count, bottom_act, bottom_cot)
+    )(*(pltpu.with_memory_space_constraint(a, pltpu.HBM) for a in (ids, emb, slot_row, slot_count, bottom_act, bottom_cot)))
     freq_grad, table_grad, weight_grad, bias_row = pl.pallas_call(
         finish_kernel,
         out_shape=(

time: 95.5 us -> 77.9 us (0.82)
  Pallas kernels: 89.7 us -> 77.1 us
  local copies, waits for them, and re-layouts: 4.8 us -> 0 us
    pallas_call x1, Pallas kernels: 87.3 us -> 74.8 us  [per_device(): pl.pallas_call(main_kernel, out_shape=(pltpu.VMEM((2, NX, R1, 128), F32),...]
    unnamed x12 -> x0, local copies, waits for them, and re-layouts: 4.8 us -> none
where the time goes in v2:
time: 77.9 us; the launch traced here: 77.8 us
  Pallas kernels  77.1 us (99%)
    pallas_call x1, Pallas kernels, per_device(): pl.pallas_call(main_kernel, out_shape=(pltpu.VMEM((2, NX, R1, 128), F32),...  74.8 us
    pallas_call x1, Pallas kernels, per_device(): pl.pallas_call(finish_kernel, out_shape=(jax.ShapeDtypeStruct((FREQ, 128)...  2.36 us

profile of v2, /device:TPU:1, one launch (start us, length us, event | category | flops | bytes accessed | tf_op | source)
XLA Modules:
  0.0 77.8 jit_solution(8585333141656787817)
XLA Ops:
  0.6 74.8 %shard_map.93 = (f32[2,4,576,128]{3,2,1,0:T(8,128)S(1)}, f32[2048,128]{1,0:T(8,128)S(1)}) custom-call(s32[26,128]{1,0:T(8,128)} %bitcast.6, bf16[3328,128]{1,0:T(8,128)(2,1)} %bitcast.5, s32[1,1024]{1,0:T(1,128)} %slot_row_in.1, s32[1,8]{1,0:T(1,128)} %counts_in.1, bf16[128,256]{1,0:T(8,128)(2,1)} %act_in.1, bf16[128,128]{1,0:T(8,128)(2,1)} %cot_in.1), custom_call_target="tpu_custom_call" | custom-call | tf_op jit(solution)/shard_map/pallas_call | solution.py:310
  75.4 2.4 %shard_map.94 = (f32[4096,128]{1,0:T(8,128)}, f32[2048,128]{1,0:T(8,128)}, f32[256,128]{1,0:T(8,128)}, f32[1,128]{1,0:T(1,128)}) custom-call(f32[2,4,576,128]{3,2,1,0:T(8,128)S(1)} %get-tuple-element.10.g_ref, f32[2048,128]{1,0:T(8,128)S(1)} %get-tuple-element.11.table_in), custom_call_target="tpu_custom_call" | custom-call | tf_op jit(solution)/shard_map/pallas_call | solution.py:344

commit v3 on v2

--- a/solution.py
+++ b/solution.py
@@ -232,7 +232,37 @@
         t72[k * R3 : (k + 1) * R3, :] = gz[k]
 
     g_ref[c, x, rows_y(y), :] = t72[...]
-    yg_copies = [copy(t72, g_ref.at[c, x, rows_y(y)], to_y(d)) for d in order_y]
+    yg_copies = {d: copy(t72, g_ref.at[c, x, rows_y(y)], to_y(d)) for d in order_y}
+
+    before, after, far = (x + NX - 1) % NX, (x + 1) % NX, (x + 2) % NX
+    near_first = order_y[::-1]
+    pieces = [y] + [(y - d + NY) % NY for d in near_first]
+
+    def pass_on(xs, rows, target):
+        return copy(g_ref.at[c, xs, rows], g_ref.at[c, xs, rows], target)
+
+    def whole(xs):
+        return copy(g_ref.at[c, xs], g_ref.at[c, xs], to_c)
+
+    up, down, relayed = [], [], []
+
+    def spread(n):
+        for k in range(len(up), n):
+            if k > 0:
+                yg_copies[near_first[k - 1]].wait_recv()
+            up.append(pass_on(x, rows_y(pieces[k]), to_x(1)))
+            down.append(pass_on(x, rows_y(pieces[k]), to_x(3)))
+
+    def relay(n):
+        for k in range(len(relayed), n):
+            if k % 2 == 0:
+                up[k].wait_recv()
+                relayed.append(pass_on(before, rows_y(pieces[k]), to_x(1)))
+            else:
+                down[k].wait_recv()
+                relayed.append(pass_on(after, rows_y(pieces[k]), to_x(3)))
+
+    spread(1)
 
     for cp in a_copies:
         cp.wait_recv()
@@ -252,34 +282,29 @@
         acc = jnp.dot(lhs, rhs[0:SLOTS, :], preferred_element_type=F32)
         table_ref[pl.ds(pl.multiple_of(b * BLK, BLK), BLK), :] = acc[:, 0:128] + acc[:, 128:256]
 
-    for cp in yg_copies:
-        cp.wait_recv()
-
-    def pass_on(xs, rows, target):
-        return copy(g_ref.at[c, xs, rows], g_ref.at[c, xs, rows], target)
-
-    before, after, far = (x + NX - 1) % NX, (x + 1) % NX, (x + 2) % NX
-    up_a = pass_on(x, half_a, to_x(1))
-    down_b = pass_on(x, half_b, to_x(3))
-    up_b = pass_on(x, half_b, to_x(1))
-    down_a = pass_on(x, half_a, to_x(3))
-    cg_copies = [copy(g_ref.at[c, x], g_ref.at[c, x], to_c)]
-    up_a.wait_recv()
-    far_a = pass_on(before, half_a, to_x(1))
-    down_b.wait_recv()
-    far_b = pass_on(after, half_b, to_x(3))
-    cg_copies.append(pass_on(before, half_a, to_c))
-    cg_copies.append(pass_on(after, half_b, to_c))
-    for cp, xs, rows in ((up_b, before, half_b), (down_a, after, half_a), (far_a, far, half_a), (far_b, far, half_b)):
-        cp.wait_recv()
-        cg_copies.append(pass_on(xs, rows, to_c))
+    spread(5)
+    relay(1)
+    spread(7)
+    relay(3)
+    spread(8)
+    cg_copies = [whole(x)]
+    relay(8)
+    for k in range(1, NY, 2):
+        up[k].wait_recv()
+    cg_copies.append(whole(before))
+    for k in range(0, NY, 2):
+        down[k].wait_recv()
+    cg_copies.append(whole(after))
+    for cp in relayed:
+        cp.wait_recv()
+    cg_copies.append(whole(far))
     for cp in cg_copies:
         cp.wait_recv()
     for cp in sends:
         cp.wait_send()
 
 
-N_COPIES = NX + 6 + 3 * (NY - 1) + 2 * (NZ - 1) + 6 + 7
+N_COPIES = NX + 6 + 3 * (NY - 1) + 2 * (NZ - 1) + 3 * NY + NX
 
 
 def finish_kernel(g_ref, table_in, freq_ref, table_ref, weight_ref, bias_ref, sem):

time: 77.9 us -> 77.6 us (level); the launches traced: 77.8 us -> 76.3 us
  Pallas kernels: 77.1 us -> 75.6 us
    pallas_call x1, Pallas kernels: 74.8 us -> 73.3 us  [per_device(): pl.pallas_call(main_kernel, out_shape=(pltpu.VMEM((2, NX, R1, 128), F32),...]
where the time goes in v3:
time: 77.6 us; the launch traced here: 76.3 us
  Pallas kernels  75.6 us (97%)
    pallas_call x1, Pallas kernels, per_device(): pl.pallas_call(main_kernel, out_shape=(pltpu.VMEM((2, NX, R1, 128), F32),...  73.3 us
    pallas_call x1, Pallas kernels, per_device(): pl.pallas_call(finish_kernel, out_shape=(jax.ShapeDtypeStruct((FREQ, 128)...  2.36 us

profile of v3, /device:TPU:1, one launch (start us, length us, event | category | flops | bytes accessed | tf_op | source)
XLA Modules:
  0.0 76.3 jit_solution(13145973848693182413)
XLA Ops:
  0.6 73.3 %shard_map.93 = (f32[2,4,576,128]{3,2,1,0:T(8,128)S(1)}, f32[2048,128]{1,0:T(8,128)S(1)}) custom-call(s32[26,128]{1,0:T(8,128)} %bitcast.6, bf16[3328,128]{1,0:T(8,128)(2,1)} %bitcast.5, s32[1,1024]{1,0:T(1,128)} %slot_row_in.1, s32[1,8]{1,0:T(1,128)} %counts_in.1, bf16[128,256]{1,0:T(8,128)(2,1)} %act_in.1, bf16[128,128]{1,0:T(8,128)(2,1)} %cot_in.1), custom_call_target="tpu_custom_call" | custom-call | tf_op jit(solution)/shard_map/pallas_call | solution.py:335
  73.9 2.4 %shard_map.94 = (f32[4096,128]{1,0:T(8,128)}, f32[2048,128]{1,0:T(8,128)}, f32[256,128]{1,0:T(8,128)}, f32[1,128]{1,0:T(1,128)}) custom-call(f32[2,4,576,128]{3,2,1,0:T(8,128)S(1)} %get-tuple-element.10.g_ref, f32[2048,128]{1,0:T(8,128)S(1)} %get-tuple-element.11.table_in), custom_call_target="tpu_custom_call" | custom-call | tf_op jit(solution)/shard_map/pallas_call | solution.py:369

commit v4 on v3

--- a/solution.py
+++ b/solution.py
@@ -59,26 +59,32 @@
 
     g = lax.axis_index("grp")
     y = lax.axis_index("own")
-    x = g // (2 * NZ)
-    z = (g // 2) % NZ
-    c = g % 2
+    x = lax.div(g, 2 * NZ)
+    z = lax.rem(lax.div(g, 2), NZ)
+    c = lax.rem(g, 2)
 
     def dev(xx, yy, zz, cc):
         return (xx * (2 * NZ) + zz * 2 + cc, yy)
 
     def to_x(d):
-        return dev((x + d) % NX, y, z, c)
+        return dev(lax.rem(x + d, NX), y, z, c)
 
     def to_y(d):
-        return dev(x, (y + d) % NY, z, c)
+        return dev(x, lax.rem(y + d, NY), z, c)
 
     def to_z(d):
-        return dev(x, y, (z + d) % NZ, c)
+        return dev(x, y, lax.rem(z + d, NZ), c)
 
     to_c = dev(x, y, z, 1 - c)
 
     used = [0]
     sends = []
+    waited = [0]
+
+    def drain(upto):
+        while waited[0] < upto:
+            sends[waited[0]].wait_send()
+            waited[0] += 1
 
     def copy(src, dst, target):
         i = used[0]
@@ -151,7 +157,7 @@
             x_copies[3] = copy(rc.at[3, half_a], rx.at[3], to_x(3))
 
     for k, o in enumerate(order):
-        px = (x + o) % NX
+        px = lax.rem(x + o, NX)
 
         @pl.loop(0, FX // BLK)
         def _(b, o=o, px=px):
@@ -205,7 +211,7 @@
     def rows_y(k):
         return pl.ds(pl.multiple_of(k * R2, 8), R2)
 
-    y_copies = [copy(s1.at[rows_y((y + d) % NY)], ry.at[d - 1], to_y(d)) for d in order_y]
+    y_copies = [copy(s1.at[rows_y(lax.rem(y + d, NY))], ry.at[d - 1], to_y(d)) for d in order_y]
 
     for cp in y_copies:
         cp.wait_recv()
@@ -215,8 +221,9 @@
     for k in range(NZ):
         s2z[k] = s2[k * R3 : (k + 1) * R3, :]
 
-    z_copies = [copy(s2z.at[(z + d) % NZ], rz.at[d - 1], to_z(d)) for d in order_z]
-    a_copies = [copy(sg.at[(y + d) % NY], ra.at[d], to_y(d)) for d in order_y]
+    z_copies = [copy(s2z.at[lax.rem(z + d, NZ)], rz.at[d - 1], to_z(d)) for d in order_z]
+    n_reduce = len(sends)
+    a_copies = [copy(sg.at[lax.rem(y + d, NY)], ra.at[d], to_y(d)) for d in order_y]
     ra[0] = sg[y]
     for cp in z_copies:
         cp.wait_recv()
@@ -226,17 +233,19 @@
     gz[z] = s3
     zg_copies = [copy(gz.at[z], gz.at[z], to_z(d)) for d in order_z]
 
+    drain(n_reduce)
     for cp in zg_copies:
         cp.wait_recv()
     for k in range(NZ):
         t72[k * R3 : (k + 1) * R3, :] = gz[k]
 
+    n_z = len(sends)
     g_ref[c, x, rows_y(y), :] = t72[...]
     yg_copies = {d: copy(t72, g_ref.at[c, x, rows_y(y)], to_y(d)) for d in order_y}
 
-    before, after, far = (x + NX - 1) % NX, (x + 1) % NX, (x + 2) % NX
+    before, after, far = lax.rem(x + NX - 1, NX), lax.rem(x + 1, NX), lax.rem(x + 2, NX)
     near_first = order_y[::-1]
-    pieces = [y] + [(y - d + NY) % NY for d in near_first]
+    pieces = [y] + [lax.rem(y - d + NY, NY) for d in near_first]
 
     def pass_on(xs, rows, target):
         return copy(g_ref.at[c, xs, rows], g_ref.at[c, xs, rows], target)
@@ -272,16 +281,21 @@
         rhs[d * CAP : (d + 1) * CAP, 0:128] = top
         rhs[d * CAP : (d + 1) * CAP, 128:256] = (v - top.astype(F32)).astype(BF16)
 
-    @pl.loop(0, ROWS_OWN // BLK)
-    def _(b):
-        cols = []
-        for d in range(NY):
-            rel = relative(ra[d, CAP : CAP + 8, :].astype(jnp.int32), b * BLK, BLK)
-            cols.append(onehot_bf16(rel[0:1, :], iota_bf))
-        lhs = jnp.concatenate(cols, axis=1)
-        acc = jnp.dot(lhs, rhs[0:SLOTS, :], preferred_element_type=F32)
-        table_ref[pl.ds(pl.multiple_of(b * BLK, BLK), BLK), :] = acc[:, 0:128] + acc[:, 128:256]
-
+    drain(n_z)
+
+    def scatter(lower, upper):
+        @pl.loop(lower, upper)
+        def _(b):
+            cols = []
+            for d in range(NY):
+                rel = relative(ra[d, CAP : CAP + 8, :].astype(jnp.int32), b * BLK, BLK)
+                cols.append(onehot_bf16(rel[0:1, :], iota_bf))
+            lhs = jnp.concatenate(cols, axis=1)
+            acc = jnp.dot(lhs, rhs[0:SLOTS, :], preferred_element_type=F32)
+            table_ref[pl.ds(pl.multiple_of(b * BLK, BLK), BLK), :] = acc[:, 0:128] + acc[:, 128:256]
+
+    blocks = ROWS_OWN // BLK
+    scatter(0, blocks // 2)
     spread(5)
     relay(1)
     spread(7)
@@ -295,13 +309,14 @@
     for k in range(0, NY, 2):
         down[k].wait_recv()
     cg_copies.append(whole(after))
+    scatter(blocks // 2, blocks)
+    drain(n_z + (NY - 1) + 2 * NY)
     for cp in relayed:
         cp.wait_recv()
     cg_copies.append(whole(far))
     for cp in cg_copies:
         cp.wait_recv()
-    for cp in sends:
-        cp.wait_send()
+    drain(len(sends))
 
 
 N_COPIES = NX + 6 + 3 * (NY - 1) + 2 * (NZ - 1) + 3 * NY + NX
@@ -316,10 +331,9 @@
         cps.append(cp)
 
     for h in range(2):
-        for k in range(NX):
-            copy(g_ref.at[h, k, 0:FX], freq_ref.at[pl.ds(h * HALF + k * FX, FX)])
-            copy(g_ref.at[h, k, FX : FX + WX], weight_ref.at[pl.ds(h * 128 + k * WX, WX)])
+        copy(g_ref.at[h, :, 0:FX], freq_ref.at[h])
     copy(table_in, table_ref)
+    copy(g_ref.at[:, :, FX : FX + WX], weight_ref)
     bias_ref[...] = g_ref[0, 0, FX + WX : FX + WX + 1, :]
     for cp in cps:
         cp.wait()
@@ -369,20 +383,20 @@
     freq_grad, table_grad, weight_grad, bias_row = pl.pallas_call(
         finish_kernel,
         out_shape=(
-            jax.ShapeDtypeStruct((FREQ, 128), F32),
+            jax.ShapeDtypeStruct((2, NX, FX, 128), F32),
             jax.ShapeDtypeStruct((ROWS_OWN, 128), F32),
-            jax.ShapeDtypeStruct((256, 128), F32),
+            jax.ShapeDtypeStruct((2, NX, WX, 128), F32),
             jax.ShapeDtypeStruct((1, 128), F32),
         ),
         in_specs=[vm, vm],
         out_specs=(anym, anym, anym, vm),
-        scratch_shapes=[pltpu.SemaphoreType.DMA((4 * NX + 1,))],
+        scratch_shapes=[pltpu.SemaphoreType.DMA((4,))],
         compiler_params=pltpu.CompilerParams(vmem_limit_bytes=4 * 2**20),
     )(
         pltpu.with_memory_space_constraint(gathered, pltpu.VMEM),
         pltpu.with_memory_space_constraint(table, pltpu.VMEM),
     )
-    return freq_grad, table_grad, weight_grad, bias_row.reshape(128)
+    return freq_grad.reshape(FREQ, 128), table_grad, weight_grad.reshape(256, 128), bias_row.reshape(128)
 
 
 def solution(mesh):

time: 77.6 us -> 77.4 us (level)
  no operation moved by 1% of the time
where the time goes in v4:
time: 77.4 us; the launch traced here: 76 us
  Pallas kernels  75.3 us (97%)
    pallas_call x1, Pallas kernels, per_device(): pl.pallas_call(main_kernel, out_shape=(pltpu.VMEM((2, NX, R1, 128), F32),...  73.1 us
    pallas_call x1, Pallas kernels, per_device(): pl.pallas_call(finish_kernel, out_shape=(jax.ShapeDtypeStruct((2, NX, FX,...  2.24 us

profile of v4, /device:TPU:1, one launch (start us, length us, event | category | flops | bytes accessed | tf_op | source)
XLA Modules:
  0.0 76.0 jit_solution(5669052202813733063)
XLA Ops:
  0.6 73.1 %shard_map.93 = (f32[2,4,576,128]{3,2,1,0:T(8,128)S(1)}, f32[2048,128]{1,0:T(8,128)S(1)}) custom-call(s32[26,128]{1,0:T(8,128)} %bitcast.8, bf16[3328,128]{1,0:T(8,128)(2,1)} %bitcast.7, s32[1,1024]{1,0:T(1,128)} %slot_row_in.1, s32[1,8]{1,0:T(1,128)} %counts_in.1, bf16[128,256]{1,0:T(8,128)(2,1)} %act_in.1, bf16[128,128]{1,0:T(8,128)(2,1)} %cot_in.1), custom_call_target="tpu_custom_call" | custom-call | tf_op jit(solution)/shard_map/pallas_call | solution.py:349
  73.7 2.2 %shard_map.94 = (f32[2,4,512,128]{3,2,1,0:T(8,128)}, f32[2048,128]{1,0:T(8,128)}, f32[2,4,32,128]{3,2,1,0:T(8,128)}, f32[1,128]{1,0:T(1,128)}) custom-call(f32[2,4,576,128]{3,2,1,0:T(8,128)S(1)} %get-tuple-element.10.g_ref, f32[2048,128]{1,0:T(8,128)S(1)} %get-tuple-element.11.table_in), custom_call_target="tpu_custom_call" | custom-call | tf_op jit(solution)/shard_map/pallas_call | solution.py:383
